TPU v7x, 1024 devices: a whole 8x8x8 slice. The times are simulated.
1024 devices in a mesh: dp: 8 (over y), fsdp: 16 (over z, core), tensor: 8 (over x).
Axes of the slice: x: 8, y: 8, z: 8, core: 2. Of those that a mesh axis runs over, the one named last changes fastest.
Arguments:
- momentum: float32 [8192, 28672], P('fsdp', 'tensor'), may hold values from -180 to 180, as said below
- previous: bfloat16 [28672, 128], P('tensor'), may hold values from -6 to 6
Outputs:
- left_factor: float32 [8192, 128], P('fsdp')
- right_factor: bfloat16 [28672, 128], P('tensor')
- column_scale: float32 [128], replicated
Inputs may be any that keep to these rules, and one draw needn't show every extreme that they name: momentum entries are finite.
All inputs are finite; a program needn't handle non-finite values.
Results may differ from a plain program's by a relative error of at most 0.00055.
Values may be sent and summed in bfloat16 or wider, within the bound.
A program may use at most 32 MiB of HBM per device.

v0:
```python
import math

import jax
import jax.numpy as jnp
from jax import lax
from jax.sharding import PartitionSpec as P

NR = 8192
NC = 28672


def whiten(matrix, lower_factor):
    return lax.linalg.triangular_solve(
        lower_factor, matrix, left_side=False, lower=True, transpose_a=True
    )


def shards(momentum, previous):
    partial_power = jnp.dot(momentum, previous.astype(jnp.float32), precision=lax.Precision.HIGHEST)
    power = lax.psum(partial_power, "tensor")
    gram = lax.psum(jnp.dot(power.T, power, precision=lax.Precision.HIGHEST), "fsdp")
    lower_factor = jnp.linalg.cholesky(gram)
    ortho = whiten(power, lower_factor)
    scattered = lax.psum_scatter(
        jnp.dot(momentum.T, ortho, precision=lax.Precision.HIGHEST),
        "fsdp",
        scatter_dimension=0,
        tiled=True,
    )
    squares_local = jnp.sum(scattered * scattered, axis=0)
    totals = lax.psum(squares_local, ("fsdp", "tensor"))
    column = jnp.sqrt(totals + 1e-06)
    right_share = (scattered * (math.sqrt(NC) / column)).astype(jnp.bfloat16)
    right_whole = lax.all_gather(right_share, "fsdp", axis=0, tiled=True)
    return (ortho * math.sqrt(NR), right_whole, column / math.sqrt(NC))


def solution(mesh):
    placed = (P("fsdp", "tensor"), P("tensor", None))
    return jax.shard_map(
        shards,
        mesh=mesh,
        in_specs=placed,
        out_specs=(P("fsdp", None), P("tensor", None), P()),
        check_vma=False,
    )
```

profile of v0, /device:TPU:1, one launch (start us, length us, event | category | flops | bytes accessed | tf_op | source)
XLA Modules:
  0.0 599.2 jit_solution(8240675309328615516)
XLA Ops:
  7.2 0.0 copy-start
  7.2 0.0 all-reduce.3.cloned.1.call-start
  7.2 1.1 copy-done
  8.3 6.2 %fusion.4 = f32[512,128]{1,0:T(8,128)} fusion(f32[512,3584]{1,0:T(8,128)} %param.2, bf16[3584,128]{1,0:T(8,128)(2,1)S(1)} %copy-done), kind=kOutput, calls=%fused_computation.17 | convolution fusion | flops 2818572288 | bytes 8519680 | tf_op jit(solution)/shard_map/dot_general | solution.py:19
  14.6 0.0 all-reduce.3.cloned.1.call-update
  14.6 0.0 all-reduce.5.cloned.1.call-start
  14.6 90.7 %all-reduce.3.cloned.1.call-done = f32[512,128]{1,0:T(8,128)} async-done(((f32[512,128]{1,0:T(8,128)}), f32[512,128]{1,0:T(8,128)}) %all-reduce.3.cloned.1.call-update) | async-done | bytes 262160 | tf_op jit(solution)/shard_map/psum | solution.py:20
  105.3 2.2 fusion.5
  107.6 0.0 all-reduce.5.cloned.1.call-update
  107.6 0.0 reduce-scatter.4.cloned.1.call-start
  107.7 116.7 %all-reduce.5.cloned.1.call-done = f32[128,128]{0,1:T(8,128)} async-done(((f32[128,128]{0,1:T(8,128)}), f32[128,128]{0,1:T(8,128)}) %all-reduce.5.cloned.1.call-update) | async-done | bytes 65552 | tf_op jit(solution)/shard_map/psum | solution.py:21
  224.4 0.9 copy.12
  225.3 0.9 fusion.3
  226.2 11.7 %cholesky.16 = f32[128,128]{1,0:T(8,128)S(1)} custom-call(f32[128,128]{1,0:T(8,128)S(1)} %fusion.3), custom_call_target="Cholesky" | custom-call | tf_op jit(solution)/shard_map/jit(cholesky)/cholesky | solution.py:22
  237.9 0.6 compare_reduce_fusion
  238.6 0.7 fusion
  239.2 9.8 %custom-call.6 = f32[1,128,128]{1,2,0:T(8,128)S(1)} custom-call(f32[1,128,128]{2,1,0:T(8,128)S(1)} %fusion), custom_call_target="InvertDiagBlocksLowerTriangular" | custom-call | tf_op jit(solution)/shard_map/triangular_solve | solution.py:13
  249.1 2.0 broadcast_multiply_fusion
  251.1 6.0 convolution_bitcast_fusion
  257.1 1.7 copy.15
  258.8 0.0 reduce-scatter.4.cloned.1.call-update
  258.8 60.8 %reduce-scatter.4.cloned.1.call-done = f32[224,128]{1,0:T(8,128)} async-done(((f32[3584,128]{1,0:T(8,128)}), f32[224,128]{1,0:T(8,128)}) %reduce-scatter.4.cloned.1.call-update) | async-done | bytes 114704 | tf_op jit(solution)/shard_map/reduce_scatter | solution.py:24
  319.6 1.0 copy.16
  320.6 0.1 multiply_reduce_fusion
  320.7 243.4 %psum.23 = f32[128]{0:T(128)S(1)} all-reduce(f32[128]{0:T(128)S(1)} %multiply_reduce_fusion), channel_id=1, replica_groups=mesh['dp'=8,'fsdp'=16,'tensor'=8] {'fsdp','tensor'}, use_global_device_ids=true, to_apply=%region_6.7 | all-reduce | flops 128 | bytes 1024 | tf_op jit(solution)/shard_map/psum | solution.py:31
  564.2 0.5 broadcast_multiply_fusion.1
  564.7 0.9 multiply_convert_fusion
  565.6 26.2 %all_gather.3 = bf16[3584,128]{1,0:T(8,128)(2,1)S(1)} all-gather(bf16[224,128]{1,0:T(8,128)(2,1)S(1)} %multiply_convert_fusion), channel_id=1, replica_groups=mesh['dp'=8,'fsdp'=16,'tensor'=8] {'fsdp'}, dimensions={0}, use_global_device_ids=true | all-gather | bytes 974848 | tf_op jit(solution)/shard_map/all_gather | solution.py:34
  591.8 0.9 copy.20
  (1 shorter events, 0.0 us)
Async XLA Ops:
  7.2 1.2 copy-start
  7.2 98.2 %all-reduce.3.cloned.1.call-start = ((), (), s32[]{:S(2)}) async-start(), calls=%async_computation.1 | async-start | bytes 524288 | tf_op jit(solution)/shard_map/psum | solution.py:20
  14.6 209.8 %all-reduce.5.cloned.1.call-start = ((), (), s32[]{:S(2)}) async-start(), calls=%async_computation.2 | async-start | bytes 131072 | tf_op jit(solution)/shard_map/psum | solution.py:21
  107.6 212.0 %reduce-scatter.4.cloned.1.call-start = ((), (), s32[]{:S(2)}) async-start(), calls=%async_computation.3 | async-start | bytes 1949696 | tf_op jit(solution)/shard_map/reduce_scatter | solution.py:24
Sparse Core Ops, SparseCore 0:
  14.7 90.5 all-reduce.2
  108.3 116.0 all-reduce.4
  258.9 60.6 reduce-scatter.3
where the time goes:
time: 600 us; the launch traced here: 599 us
  blocking collectives  270 us (45%)
  waiting for transfers between devices  268 us (45%)
  other arithmetic  25.2 us (4%)
  matrix products  16.4 us (3%)
  between operations  13.8 us (2%)
    psum x1, blocking collectives, shards(): totals = lax.psum(squares_local, ('fsdp', 'tensor'))  243 us
    psum x1, waiting for transfers between devices, shards(): lax.psum(jnp.dot(power.T, power, precision=lax.Precision.HIGHEST), 'fsdp')  117 us
    psum x1, waiting for transfers between devices, shards(): power = lax.psum(partial_power, 'tensor')  90.7 us
    reduce_scatter x1, waiting for transfers between devices, shards(): lax.psum_scatter(jnp.dot(momentum.T, ortho, precision=lax.Precision.HIGHE...  60.8 us
    all_gather x1, blocking collectives, shards(): right_whole = lax.all_gather(right_share, 'fsdp', axis=0, tiled=True)  26.2 us
    another operation x3, other arithmetic, shards(): lower_factor = jnp.linalg.cholesky(gram)  12.4 us
  transfers between devices with their start and end apart: 3, of which 3 were waited for; matrix products, arithmetic and copies ran while one was open for 0% of the time, Pallas kernels for 0%

commit v1 on v0

v1 whole, which is shorter than its diff:
```python
import functools
import math

import jax
import jax.numpy as jnp
from jax import lax
from jax.experimental import pallas as pl
from jax.experimental.pallas import tpu as pltpu
from jax.sharding import PartitionSpec as P

HIGHEST = lax.Precision.HIGHEST
MESH = pl.DeviceIdType.MESH
RANK = 128
F32 = jnp.float32


def aligned(value, multiple=8):
    return pl.multiple_of(value, multiple)


def invert_cholesky(a_ref, linv_ref):
    shape = (8, RANK)
    sub = lax.broadcasted_iota(jnp.int32, shape, 0)
    lane = lax.broadcasted_iota(jnp.int32, shape, 1)

    def row_of(v, p):
        return jnp.broadcast_to(v[p : p + 1, :], shape)

    def block(k, carry):
        off = aligned(k * 8)
        rows = a_ref[pl.ds(off, 8), :]
        turned = pltpu.roll(rows, lax.rem(RANK - off, RANK), 1)
        cols = [jnp.broadcast_to(turned[:, q : q + 1], shape) for q in range(8)]
        rel = lane - off
        scale = jnp.zeros(shape, F32)
        for p in range(8):
            pivot = row_of(cols[p], p)
            factor = jnp.where(sub > p, cols[p] * (1.0 / pivot), 0.0)
            pivot_row = row_of(rows, p)
            for q in range(p + 1, 8):
                cols[q] = cols[q] - factor * row_of(cols[q], p)
            rows = jnp.where((rel == p) & (sub > p), 0.0, rows) - factor * jnp.where(rel == p, 1.0, pivot_row)
            scale = jnp.where(sub == p, lax.rsqrt(pivot), scale)
        panel = jnp.where(rel == sub, 1.0, rows) * scale
        panel = jnp.where((rel > sub) & (rel < 8), 0.0, panel)
        linv_ref[pl.ds(off, 8), :] = jnp.where(rel <= sub, panel, 0.0)
        upper = jnp.where(rel >= 8, panel, 0.0)
        update = lax.dot_general(
            upper, panel, (((0,), (0,)), ((), ())), precision=HIGHEST, preferred_element_type=F32
        )
        row = lax.broadcasted_iota(jnp.int32, (RANK, RANK), 0)
        col = lax.broadcasted_iota(jnp.int32, (RANK, RANK), 1) - off
        a = a_ref[...]
        a_ref[...] = jnp.where(
            row >= off + 8, jnp.where((col >= 0) & (col < 8), 0.0, a) - update, a
        )
        return carry

    lax.fori_loop(0, RANK // 8, block, 0)


def body(
    sizes, m_ref, p_ref, left_ref, right_ref, column_ref,
    p_v, mrow, mcol, wpart, rsw, wfull, gpart, rsg, gfull, work, linv, zpart, rsz, zfull, nsend, nrecv, nrow, nplane,
    load_sem, send_sem, recv_sem,
):
    dn, fn, tn, nr, nc = sizes
    zn = fn // 2
    mr, mc = m_ref.shape
    wr = mr // dn
    br = wr // tn
    cy = mc // dn
    cz = cy // zn
    cores = ((0, (cz // 16 + 1) * 8), ((cz // 16 + 1) * 8, cz - (cz // 16 + 1) * 8))
    gr = RANK // fn
    width = mcol.shape[1]
    y, f, x = lax.axis_index("dp"), lax.axis_index("fsdp"), lax.axis_index("tensor")
    z, c = f // 2, lax.rem(f, 2)

    def at(dy=0, df=0, dx=0):
        return (lax.rem(y + dy, dn), lax.rem(f + df, fn), lax.rem(x + dx, tn))

    def send(src, dst, phase, device):
        pltpu.make_async_remote_copy(
            src_ref=src, dst_ref=dst, send_sem=send_sem.at[phase], recv_sem=recv_sem.at[phase],
            device_id=device, device_id_type=MESH,
        ).start()

    def wait(ref, sem):
        pltpu.make_async_copy(ref, ref, sem).wait()

    def by_core(fun):
        for core, (start, length) in enumerate(cores):
            pl.when(c == core)(functools.partial(fun, start, length))

    lines_x = [at(dx=i) for i in range(1, tn)]
    lines_f = [at(df=i) for i in range(1, fn)]
    plane = [at(dy=i, dx=j) for i in range(dn) for j in range(tn) if i or j]

    barrier = pltpu.get_barrier_semaphore()
    for device in plane + lines_f:
        pl.semaphore_signal(barrier, inc=1, device_id=device, device_id_type=MESH)

    first_col = (cy * y) // 128 * 128
    skip = aligned(cy * y - first_col)
    load_p = pltpu.make_async_copy(p_ref, p_v, load_sem.at[0])
    load_row = pltpu.make_async_copy(m_ref.at[pl.ds(aligned(wr * y), wr)], mrow, load_sem.at[1])
    load_col = pltpu.make_async_copy(
        m_ref.at[:, pl.ds(aligned(first_col, 128), width)], mcol, load_sem.at[2]
    )
    load_p.start()
    load_row.start()
    load_col.start()
    load_p.wait()
    load_row.wait()

    step = 512 if mc % 512 == 0 else 128

    def power_step(i, total):
        at_k = aligned(i * step, 128)
        m = mrow[:, pl.ds(at_k, step)]
        first = m.astype(jnp.bfloat16)
        rest = m - first.astype(F32)
        second = rest.astype(jnp.bfloat16)
        third = (rest - second.astype(F32)).astype(jnp.bfloat16)
        terms = jnp.concatenate([first, second, third], axis=0)
        return total + jnp.dot(terms, p_v[pl.ds(at_k, step), :], preferred_element_type=F32)

    terms = lax.fori_loop(0, mc // step, power_step, jnp.zeros((3 * wr, RANK), F32))
    wpart[...] = terms[:wr] + (terms[wr : 2 * wr] + terms[2 * wr :])

    pl.semaphore_wait(barrier, len(plane) + len(lines_f))

    for i, device in enumerate(lines_x):
        to = lax.rem(x + 1 + i, tn)
        send(wpart.at[pl.ds(aligned(to * br), br)], rsw.at[x], 0, device)
    rsw[x] = wpart[pl.ds(aligned(x * br), br), :]
    wait(rsw.at[pl.ds(0, tn - 1)], recv_sem.at[0])
    mine = aligned((y * tn + x) * br)
    total = rsw[0]
    for i in range(1, tn):
        total = total + rsw[i]
    wfull[pl.ds(mine, br), :] = total

    for device in plane:
        send(wfull.at[pl.ds(mine, br)], wfull.at[pl.ds(mine, br)], 1, device)
    load_col.wait()
    wait(wfull.at[pl.ds(0, mr - br)], recv_sem.at[1])

    w = wfull[...]
    gpart[...] = lax.dot_general(w, w, (((0,), (0,)), ((), ())), precision=HIGHEST, preferred_element_type=F32)
    for i, device in enumerate(lines_f):
        to = lax.rem(f + 1 + i, fn)
        send(gpart.at[pl.ds(aligned(to * gr), gr)], rsg.at[f], 2, device)
    rsg[f] = gpart[pl.ds(aligned(f * gr), gr), :]

    zpart[...] = lax.dot_general(
        mcol[...], w, (((0,), (0,)), ((), ())), precision=HIGHEST, preferred_element_type=F32
    )
    for i in range(zn):
        to_z = lax.rem(z + i, zn)
        for core, (start, length) in enumerate(cores):

            def send_part(start=start, length=length, core=core):
                send(
                    zpart.at[pl.ds(aligned(skip + to_z * cz + start), length)],
                    rsz.at[f, pl.ds(0, length)], 3, (y, 2 * to_z + core, x),
                )

            if i:
                send_part()
            else:
                pl.when(c != core)(send_part)

    wait(rsg.at[pl.ds(0, fn - 1)], recv_sem.at[2])
    total = rsg[0]
    for i in range(1, fn):
        total = total + rsg[i]
    gmine = aligned(f * gr)
    gfull[pl.ds(gmine, gr), :] = total
    for device in lines_f:
        send(gfull.at[pl.ds(gmine, gr)], gfull.at[pl.ds(gmine, gr)], 4, device)

    block = y * zn + z

    def share(start, length):
        rsz[f, pl.ds(0, length)] = zpart[pl.ds(aligned(skip + z * cz + start), length), :]
        wait(rsz.at[pl.ds(0, fn - 1), pl.ds(0, length)], recv_sem.at[3])
        total = rsz[0, pl.ds(0, length)]
        for i in range(1, fn):
            total = total + rsz[i, pl.ds(0, length)]
        zfull[block, pl.ds(start, length)] = total
        own = zfull.at[block, pl.ds(start, length)]
        for i in range(1, dn):
            send(own, own, 5, at(dy=i))
        for i in range(1, zn):
            send(own, own, 5, at(df=2 * i))

    by_core(share)

    wait(gfull.at[pl.ds(0, RANK - gr)], recv_sem.at[4])
    work[...] = gfull[...]
    invert_cholesky(work, linv)

    def squares(start, length):
        fb = lax.dot_general(
            zfull[block, pl.ds(start, length)], linv[...], (((1,), (1,)), ((), ())),
            precision=HIGHEST, preferred_element_type=F32,
        )
        nsend[...] = jnp.sum((fb * fb).reshape(length // 8, 8, RANK), axis=0)

    by_core(squares)
    for device in lines_f:
        send(nsend, nrecv.at[f], 6, device)
    nrecv[f] = nsend[...]

    even = lax.rem(y + z, 2)

    def forward(start, length):
        wait(zfull.at[pl.ds(0, dn + zn - 2), pl.ds(0, length)], recv_sem.at[5])
        for o in range(1, dn):

            def along_z(o=o):
                ref = zfull.at[lax.rem(y + o, dn) * zn + z, pl.ds(start, length)]
                for i in range(1, zn):
                    send(ref, ref, 7, at(df=2 * i))

            pl.when(even == o % 2)(along_z)
        for o in range(1, zn):

            def along_y(o=o):
                ref = zfull.at[y * zn + lax.rem(z + o, zn), pl.ds(start, length)]
                for i in range(1, dn):
                    send(ref, ref, 7, at(dy=i))

            pl.when(even != o % 2)(along_y)

    by_core(forward)

    left_ref[...] = lax.dot_general(
        wfull[...], linv[...] * math.sqrt(nr), (((1,), (1,)), ((), ())), precision=HIGHEST,
        preferred_element_type=F32,
    )

    wait(nrecv.at[pl.ds(0, fn - 1)], recv_sem.at[6])
    total = nrecv[0]
    for i in range(1, fn):
        total = total + nrecv[i]
    nrow[...] = jnp.sum(total, axis=0, keepdims=True)
    for device in plane:
        send(nrow, nplane.at[y * tn + x], 8, device)
    nplane[y * tn + x] = nrow[...]

    def rows_here(start, length):
        wait(zfull.at[pl.ds(0, (dn - 1) * (zn - 1)), pl.ds(0, length)], recv_sem.at[7])
        half = zfull.at[:, pl.ds(start, length)]
        send(half, half, 9, (y, f + 1 - 2 * c, x))

    by_core(rows_here)

    wait(nplane.at[pl.ds(0, dn * tn - 1)], recv_sem.at[8])
    column = jnp.sqrt(jnp.sum(nplane[...], axis=0) + 1e-06)
    column_ref[...] = column / math.sqrt(nc)
    factor = jnp.transpose(linv[...]) * (math.sqrt(nc) / column)
    work[...] = factor

    def rows_there(start, length):
        other = cz - length
        wait(zfull.at[:, pl.ds(0, other)], recv_sem.at[9])

    by_core(rows_there)

    per = 2 if cz % 16 else 1

    def finish(i, carry):
        rows = zfull[pl.ds(i * per, per)].reshape(per * cz, RANK)
        out = jnp.dot(rows, work[...], precision=HIGHEST, preferred_element_type=F32)
        right_ref[pl.ds(aligned(i * per * cz, 16), per * cz), :] = out.astype(jnp.bfloat16)
        return carry

    lax.fori_loop(0, dn * zn // per, finish, 0)

    wait(rsw.at[pl.ds(0, tn - 1)], send_sem.at[0])
    wait(wfull.at[pl.ds(0, mr - br)], send_sem.at[1])
    wait(rsg.at[pl.ds(0, fn - 1)], send_sem.at[2])
    wait(gfull.at[pl.ds(0, RANK - gr)], send_sem.at[4])
    wait(nrecv.at[pl.ds(0, fn - 1)], send_sem.at[6])
    wait(nplane.at[pl.ds(0, dn * tn - 1)], send_sem.at[8])

    def drain(start, length):
        wait(zpart.at[pl.ds(0, cy - length)], send_sem.at[3])
        wait(zfull.at[pl.ds(0, dn + zn - 2), pl.ds(0, length)], send_sem.at[5])
        wait(zfull.at[pl.ds(0, (dn - 1) * (zn - 1)), pl.ds(0, length)], send_sem.at[7])
        wait(zfull.at[:, pl.ds(0, length)], send_sem.at[9])

    by_core(drain)


def shards(sizes, momentum, previous):
    dn, fn, tn, nr, nc = sizes
    mr, mc = momentum.shape
    wr = mr // dn
    br = wr // tn
    cy = mc // dn
    zn = fn // 2
    cz = cy // zn
    most = (cz // 16 + 1) * 8
    width = -(-cy // 128) * 128
    vmem = pltpu.VMEM
    left, right, column = pl.pallas_call(
        functools.partial(body, sizes),
        out_shape=(
            jax.ShapeDtypeStruct((mr, RANK), F32),
            jax.ShapeDtypeStruct((mc, RANK), jnp.bfloat16),
            jax.ShapeDtypeStruct((1, RANK), F32),
        ),
        in_specs=[pl.BlockSpec(memory_space=pl.ANY)] * 2,
        out_specs=(pl.BlockSpec(memory_space=vmem),) * 3,
        scratch_shapes=[
            vmem((mc, RANK), jnp.bfloat16),
            vmem((wr, mc), F32),
            vmem((mr, width), F32),
            vmem((wr, RANK), F32),
            vmem((tn, br, RANK), F32),
            vmem((mr, RANK), F32),
            vmem((RANK, RANK), F32),
            vmem((fn, RANK // fn, RANK), F32),
            vmem((RANK, RANK), F32),
            vmem((RANK, RANK), F32),
            vmem((RANK, RANK), F32),
            vmem((width, RANK), F32),
            vmem((fn, most, RANK), F32),
            vmem((dn * zn, cz, RANK), F32),
            vmem((8, RANK), F32),
            vmem((fn, 8, RANK), F32),
            vmem((1, RANK), F32),
            vmem((dn * tn, 1, RANK), F32),
            pltpu.SemaphoreType.DMA((3,)),
            pltpu.SemaphoreType.DMA((10,)),
            pltpu.SemaphoreType.DMA((10,)),
        ],
        compiler_params=pltpu.CompilerParams(
            collective_id=0, has_side_effects=True, vmem_limit_bytes=40 * 2**20
        ),
    )(momentum, previous)
    return left, right, column.reshape(RANK)


def solution(mesh):
    dn, fn, tn = (mesh.shape[name] for name in ("dp", "fsdp", "tensor"))

    def run(momentum, previous):
        sizes = (dn, fn, tn, momentum.shape[0], momentum.shape[1])
        return jax.shard_map(
            functools.partial(shards, sizes),
            mesh=mesh,
            in_specs=(P("fsdp", "tensor"), P("tensor", None)),
            out_specs=(P("fsdp", None), P("tensor", None), P()),
            check_vma=False,
        )(momentum, previous)

    return run
```

time: 600 us -> 88.8 us (0.15)
  blocking collectives: 270 us -> 0 us
  waiting for transfers between devices: 268 us -> 0 us
  Pallas kernels: 0 us -> 81.5 us
  other arithmetic: 25.2 us -> 0 us
  matrix products: 16.4 us -> 0 us
  between operations: 13.8 us -> 0.65 us
    psum x1 -> x0, blocking collectives: 243 us -> none  [shards(): totals = lax.psum(squares_local, ('fsdp', 'tensor'))]
    psum x2 -> x0, waiting for transfers between devices: 207 us -> none  [the longest x1 117 us: shards(): lax.psum(jnp.dot(power.T, power, precision=lax.Precision.HIGHEST), 'fsdp')]
    pallas_call x0 -> x1, Pallas kernels: none -> 81.5 us  [shards(): pl.pallas_call(functools.partial(body, sizes), out_shape=(jax.ShapeDtypeS...]
    reduce_scatter x1 -> x0, waiting for transfers between devices: 60.8 us -> none  [shards(): lax.psum_scatter(jnp.dot(momentum.T, ortho, precision=lax.Precision.HIGHE...]
    all_gather x1 -> x0, blocking collectives: 26.2 us -> none  [shards(): right_whole = lax.all_gather(right_share, 'fsdp', axis=0, tiled=True)]
    another operation x5 -> x0, other arithmetic: 22.9 us -> none  [the longest x3 12.4 us: shards(): lower_factor = jnp.linalg.cholesky(gram)]
    dot_general x3 -> x0, matrix products: 14.4 us -> none  [the longest x1 6.21 us: shards(): jnp.dot(momentum, previous.astype(jnp.float32), precision=lax.Precision.H...]
  transfers between devices with their start and end apart: 3 -> 0, of which waited for: 3 -> 0; matrix products, arithmetic and copies ran while one was open for 0% -> 0% of each run, Pallas kernels for 0% -> 0%
where the time goes in v1:
time: 88.8 us; the launch traced here: 88.5 us
  Pallas kernels  81.5 us (92%)
  local copies, waits for them, and re-layouts  6.39 us (7%)
    pallas_call x1, Pallas kernels, shards(): pl.pallas_call(functools.partial(body, sizes), out_shape=(jax.ShapeDtypeS...  81.5 us
    unnamed x7, local copies, waits for them, and re-layouts  6.39 us

profile of v1, /device:TPU:1, one launch (start us, length us, event | category | flops | bytes accessed | tf_op | source)
XLA Modules:
  0.0 88.5 jit_solution(165641008623107560)
XLA Ops:
  0.6 0.0 copy-start
  0.6 3.1 %copy-done = f32[512,3584]{1,0:T(8,128)S(1)} copy-done((f32[512,3584]{1,0:T(8,128)S(1)}, f32[512,3584]{1,0:T(8,128)}, u32[]{:S(2)}) %copy-start) | copy-done | bytes 7340056
  3.7 0.0 copy-start.1
  3.7 1.2 %copy-done.1 = bf16[3584,128]{1,0:T(8,128)(2,1)S(1)} copy-done((bf16[3584,128]{1,0:T(8,128)(2,1)S(1)}, bf16[3584,128]{1,0:T(8,128)(2,1)}, u32[]{:S(2)}) %copy-start.1) | copy-done | bytes 917528
  4.9 81.5 %shard_map.49 = (f32[512,128]{1,0:T(8,128)S(1)}, bf16[3584,128]{1,0:T(8,128)(2,1)S(1)}, f32[1,128]{1,0:T(1,128)S(1)}) custom-call(f32[512,3584]{1,0:T(8,128)S(1)} %copy-done, bf16[3584,128]{1,0:T(8,128)(2,1)S(1)} %copy-done.1), custom_call_target="tpu_custom_call" | custom-call | tf_op jit(solution)/shard_map/pallas_call | solution.py:310
  86.4 0.7 copy.8
  87.1 0.9 %copy.9 = bf16[3584,128]{1,0:T(8,128)(2,1)} copy(bf16[3584,128]{1,0:T(8,128)(2,1)S(1)} %get-tuple-element.13) | data formatting | bytes 1835008
  88.0 0.5 copy.10
Async XLA Ops:
  0.6 3.1 %copy-start = (f32[512,3584]{1,0:T(8,128)S(1)}, f32[512,3584]{1,0:T(8,128)}, u32[]{:S(2)}) copy-start(f32[512,3584]{1,0:T(8,128)} %m_ref.1) | copy-start | bytes 22020100
  3.7 1.2 %copy-start.1 = (bf16[3584,128]{1,0:T(8,128)(2,1)S(1)}, bf16[3584,128]{1,0:T(8,128)(2,1)}, u32[]{:S(2)}) copy-start(bf16[3584,128]{1,0:T(8,128)(2,1)} %p_ref.1) | copy-start | bytes 2752516

commit v2 on v1

v2 whole, which is shorter than its diff:
```python
import functools
import math

import jax
import jax.numpy as jnp
from jax import lax
from jax.experimental import pallas as pl
from jax.experimental.pallas import tpu as pltpu
from jax.sharding import PartitionSpec as P

HIGHEST = lax.Precision.HIGHEST
MESH = pl.DeviceIdType.MESH
LIMIT = 51 * 2**20
RANK = 128
F32 = jnp.float32


def aligned(value, multiple=8):
    return pl.multiple_of(value, multiple)


STEP = 16


def split(v):
    first = v.astype(jnp.bfloat16)
    rest = v - first.astype(F32)
    second = rest.astype(jnp.bfloat16)
    return first, second, (rest - second.astype(F32)).astype(jnp.bfloat16)


def dot(a, b, ca, cb, precision=None):
    return lax.dot_general(
        a, b, (((ca,), (cb,)), ((), ())), precision=precision, preferred_element_type=F32
    )


def invert_cholesky(a_ref, linv_ref, first, last):
    shape = (STEP, RANK)
    sub = lax.broadcasted_iota(jnp.int32, shape, 0)
    lane = lax.broadcasted_iota(jnp.int32, shape, 1)
    row = lax.broadcasted_iota(jnp.int32, (RANK, RANK), 0)
    col = lax.broadcasted_iota(jnp.int32, (RANK, RANK), 1)

    def row_of(v, p):
        return jnp.broadcast_to(v[p : p + 1, :], shape)

    def block(k, carry):
        off = aligned(k * STEP, STEP)
        rows = a_ref[pl.ds(off, STEP), :]
        turned = pltpu.roll(rows, lax.rem(RANK - off, RANK), 1)
        cols = [jnp.broadcast_to(turned[:, q : q + 1], shape) for q in range(STEP)]
        rel = lane - off
        scale = jnp.zeros(shape, F32)
        for p in range(STEP):
            pivot = row_of(cols[p], p)
            factor = jnp.where(sub > p, cols[p] * (1.0 / pivot), 0.0)
            pivot_row = row_of(rows, p)
            for q in range(p + 1, STEP):
                cols[q] = cols[q] - factor * row_of(cols[q], p)
            rows = jnp.where((rel == p) & (sub > p), 0.0, rows) - factor * jnp.where(rel == p, 1.0, pivot_row)
            scale = jnp.where(sub == p, lax.rsqrt(pivot), scale)
        panel = jnp.where(rel == sub, 1.0, rows) * scale
        panel = jnp.where((rel > sub) & (rel < STEP), 0.0, panel)
        linv_ref[pl.ds(off, STEP), :] = jnp.where(rel <= sub, panel, 0.0)
        upper = jnp.where(rel >= STEP, panel, 0.0)
        u1, u2, u3 = split(upper)
        p1, p2, p3 = split(panel)
        update = dot(
            jnp.concatenate([u1, u1, u1, u2, u2, u3], axis=0),
            jnp.concatenate([p1, p2, p3, p1, p2, p1], axis=0), 0, 0,
        )
        a = a_ref[...]
        inside = (col >= off) & (col < off + STEP)
        a_ref[...] = jnp.where(row >= off + STEP, jnp.where(inside, 0.0, a) - update, a)
        return carry

    lax.fori_loop(first, last, block, 0)


def body(
    sizes, m_ref, p_ref, left_ref, fb_ref, column_ref, scale_ref,
    p_v, mrow, mcol, wpart, rsw, wfull, gpart, rsg, gfull, work, linv, zpart, rsz, zfull, nsend, nrecv, ntotal, nline,
    load_sem, send_sem, recv_sem,
):
    dn, fn, tn, nr, nc = sizes
    zn = fn // 2
    mr, mc = m_ref.shape
    wr = mr // dn
    br = wr // tn
    cy = mc // dn
    cz = cy // zn
    cores = pieces_of(cz)
    gr = RANK // fn
    width = mcol.shape[1]
    y, f, x = lax.axis_index("dp"), lax.axis_index("fsdp"), lax.axis_index("tensor")
    z, c = f // 2, lax.rem(f, 2)

    def at(dy=0, df=0, dx=0):
        return (lax.rem(y + dy, dn), lax.rem(f + df, fn), lax.rem(x + dx, tn))

    def send(src, dst, phase, device):
        pltpu.make_async_remote_copy(
            src_ref=src, dst_ref=dst, send_sem=send_sem.at[phase], recv_sem=recv_sem.at[phase],
            device_id=device, device_id_type=MESH,
        ).start()

    def wait(ref, sem):
        pltpu.make_async_copy(ref, ref, sem).wait()

    def by_core(fun, *args):
        for core in range(2):
            pl.when(c == core)(functools.partial(fun, core, *args))

    lines_x = [at(dx=i) for i in range(1, tn)]
    lines_y = [at(dy=i) for i in range(1, dn)]
    lines_f = [at(df=i) for i in range(1, fn)]
    lines_z = [at(df=2 * i) for i in range(1, zn)]
    plane = [at(dy=i, dx=j) for i in range(dn) for j in range(tn) if i or j]

    barrier = pltpu.get_barrier_semaphore()
    for device in lines_x + lines_y + lines_f:
        pl.semaphore_signal(barrier, inc=1, device_id=device, device_id_type=MESH)

    first_col = (cy * y) // 128 * 128
    skip = aligned(cy * y - first_col)
    load_p = pltpu.make_async_copy(p_ref, p_v, load_sem.at[0])
    load_row = pltpu.make_async_copy(m_ref.at[pl.ds(aligned(wr * y), wr)], mrow, load_sem.at[1])
    load_col = pltpu.make_async_copy(
        m_ref.at[:, pl.ds(aligned(first_col, 128), width)], mcol, load_sem.at[2]
    )
    load_row.start()
    load_p.start()
    load_col.start()
    load_row.wait()
    load_p.wait()

    terms = jnp.zeros((3 * wr, RANK), F32)
    step = 512 if mc % 512 == 0 else 128
    for i in range(0, mc, step):
        terms = terms + dot(
            jnp.concatenate(split(mrow[:, i : i + step]), axis=0), p_v[i : i + step, :], 1, 0
        )
    wpart[...] = terms[:wr] + (terms[wr : 2 * wr] + terms[2 * wr :])

    pl.semaphore_wait(barrier, len(lines_x) + len(lines_y) + len(lines_f))

    for i, device in enumerate(lines_x):
        to = lax.rem(x + 1 + i, tn)
        send(wpart.at[pl.ds(aligned(to * br), br)], rsw.at[x], 0, device)
    rsw[x] = wpart[pl.ds(aligned(x * br), br), :]
    wait(rsw.at[pl.ds(0, tn - 1)], recv_sem.at[0])
    mine = aligned((y * tn + x) * br)
    total = rsw[0]
    for i in range(1, tn):
        total = total + rsw[i]
    wfull[pl.ds(mine, br), :] = total

    for device in plane:
        send(wfull.at[pl.ds(mine, br)], wfull.at[pl.ds(mine, br)], 1, device)
    load_col.wait()
    wait(wfull.at[pl.ds(0, mr - br)], recv_sem.at[1])

    w = wfull[...]
    gpart[...] = dot(w, w, 0, 0, HIGHEST)
    for i, device in enumerate(lines_f):
        to = lax.rem(f + 1 + i, fn)
        send(gpart.at[pl.ds(aligned(to * gr), gr)], rsg.at[f], 2, device)
    rsg[f] = gpart[pl.ds(aligned(f * gr), gr), :]

    w1, w2, w3 = split(w)
    m1, m2, m3 = split(mcol[...])
    t1 = dot(m1, jnp.concatenate([w1, w2, w3, jnp.zeros_like(w1)], axis=1), 0, 0)
    t2 = dot(m2, jnp.concatenate([w1, w2], axis=1), 0, 0)
    t3 = t1[:, 2 * RANK : 3 * RANK] + t2[:, RANK:] + dot(m3, w1, 0, 0)
    zpart[...] = t1[:, :RANK] + (t1[:, RANK : 2 * RANK] + t2[:, :RANK] + t3)
    for piece in range(2):
        for i in range(zn):
            to_z = lax.rem(z + i, zn)
            for core in range(2):
                start, length = cores[core][piece]

                def send_part(start=start, length=length, core=core, to_z=to_z, piece=piece):
                    send(
                        zpart.at[pl.ds(aligned(skip + to_z * cz + start), length)],
                        rsz.at[piece, f, pl.ds(0, length)], 3 + piece, (y, 2 * to_z + core, x),
                    )

                if i:
                    send_part()
                else:
                    pl.when(c != core)(send_part)

    wait(rsg.at[pl.ds(0, fn - 1)], recv_sem.at[2])
    total = rsg[0]
    for i in range(1, fn):
        total = total + rsg[i]
    gmine = aligned(f * gr)
    gfull[pl.ds(gmine, gr), :] = total
    for device in lines_f:
        send(gfull.at[pl.ds(gmine, gr)], gfull.at[pl.ds(gmine, gr)], 5, device)

    block = y * zn + z

    def share(core, piece):
        start, length = cores[core][piece]
        rsz[piece, f, pl.ds(0, length)] = zpart[pl.ds(aligned(skip + z * cz + start), length), :]
        wait(rsz.at[piece, pl.ds(0, fn - 1), pl.ds(0, length)], recv_sem.at[3 + piece])
        total = rsz[piece, 0, pl.ds(0, length)]
        for i in range(1, fn):
            total = total + rsz[piece, i, pl.ds(0, length)]
        zfull[block, pl.ds(start, length)] = total
        own = zfull.at[block, pl.ds(start, length)]
        for device in lines_y + lines_z:
            send(own, own, 6 + piece, device)

    even = lax.rem(y + z, 2)

    def arrived(core, piece):
        start, length = cores[core][piece]
        wait(zfull.at[pl.ds(0, dn + zn - 2), pl.ds(0, length)], recv_sem.at[6 + piece])

    def forward(core, piece):
        start, length = cores[core][piece]
        for o in range(1, dn):

            def along_z(o=o):
                ref = zfull.at[lax.rem(y + o, dn) * zn + z, pl.ds(start, length)]
                for device in lines_z:
                    send(ref, ref, 8 + piece, device)

            pl.when(even == o % 2)(along_z)
        for o in range(1, zn):

            def along_y(o=o):
                ref = zfull.at[y * zn + lax.rem(z + o, zn), pl.ds(start, length)]
                for device in lines_y:
                    send(ref, ref, 8 + piece, device)

            pl.when(even != o % 2)(along_y)

    by_core(share, 0)
    by_core(share, 1)
    wait(gfull.at[pl.ds(0, RANK - gr)], recv_sem.at[5])
    work[...] = gfull[...]
    blocks = RANK // STEP
    invert_cholesky(work, linv, 0, blocks // 2)
    by_core(arrived, 0)
    by_core(forward, 0)
    invert_cholesky(work, linv, blocks // 2, blocks)
    by_core(arrived, 1)

    def squares(core):
        (start, first), (_, second) = cores[core]
        length = first + second
        rows = [zfull[i * zn + z, pl.ds(start, length)] for i in range(dn)]
        fb = dot(jnp.concatenate(rows, axis=0), linv[...], 1, 1, HIGHEST)
        nsend[...] = jnp.sum((fb * fb).reshape(dn * length // 8, 8, RANK), axis=0)

    by_core(squares)
    for device in lines_f:
        send(nsend, nrecv.at[f], 10, device)
    nrecv[f] = nsend[...]
    by_core(forward, 1)

    left_ref[...] = dot(wfull[...], linv[...] * math.sqrt(nr), 1, 1, HIGHEST)
    l1, l2, l3 = split(jnp.transpose(linv[...]))
    factor = jnp.concatenate([l1, l2, l3, l1, l2, l1], axis=0)

    wait(nrecv.at[pl.ds(0, fn - 1)], recv_sem.at[10])
    total = nrecv[0]
    for i in range(1, fn):
        total = total + nrecv[i]
    ntotal[...] = total
    for device in lines_x:
        send(ntotal, nline.at[x], 11, device)
    nline[x] = ntotal[...]

    other = (y, f + 1 - 2 * c, x)

    def feedback(start, length):
        rows = zfull[:, pl.ds(start, length)].reshape(dn * zn * length, RANK)
        a1, a2, a3 = split(rows)
        fb = dot(jnp.concatenate([a1, a1, a1, a2, a2, a3], axis=1), factor, 1, 0)
        fb_ref[:, pl.ds(start, length)] = fb.reshape(dn * zn, length, RANK)

    def here(core, piece):
        start, length = cores[core][piece]
        wait(zfull.at[pl.ds(0, (dn - 1) * (zn - 1)), pl.ds(0, length)], recv_sem.at[8 + piece])
        part = zfull.at[:, pl.ds(start, length)]
        send(part, part, 12 + piece, other)
        feedback(start, length)

    def there(core, piece):
        start, length = cores[1 - core][piece]
        wait(zfull.at[:, pl.ds(0, length)], recv_sem.at[12 + piece])
        feedback(start, length)

    by_core(here, 0)
    by_core(there, 0)
    by_core(here, 1)

    wait(nline.at[pl.ds(0, tn - 1)], recv_sem.at[11])
    total = nline[0]
    for i in range(1, tn):
        total = total + nline[i]
    column = jnp.sqrt(jnp.sum(total, axis=0, keepdims=True) + 1e-06)
    column_ref[...] = column / math.sqrt(nc)
    scale_ref[...] = math.sqrt(nc) / column

    by_core(there, 1)

    wait(rsw.at[pl.ds(0, tn - 1)], send_sem.at[0])
    wait(wfull.at[pl.ds(0, mr - br)], send_sem.at[1])
    wait(rsg.at[pl.ds(0, fn - 1)], send_sem.at[2])
    wait(gfull.at[pl.ds(0, RANK - gr)], send_sem.at[5])
    wait(nrecv.at[pl.ds(0, fn - 1)], send_sem.at[10])
    wait(nline.at[pl.ds(0, tn - 1)], send_sem.at[11])

    def drain(core, piece):
        _, length = cores[core][piece]
        whole = zn * (cores[0][piece][1] + cores[1][piece][1])
        wait(zpart.at[pl.ds(0, whole - length)], send_sem.at[3 + piece])
        wait(zfull.at[pl.ds(0, dn + zn - 2), pl.ds(0, length)], send_sem.at[6 + piece])
        wait(zfull.at[pl.ds(0, (dn - 1) * (zn - 1)), pl.ds(0, length)], send_sem.at[8 + piece])
        wait(zfull.at[:, pl.ds(0, length)], send_sem.at[12 + piece])

    for piece in range(2):
        by_core(drain, piece)


def pieces_of(rows):
    first = (rows // 16 + 1) * 8
    out = []
    for start, length in ((0, first), (first, rows - first)):
        half = (length // 2 + 7) // 8 * 8
        out.append(((start, half), (start + half, length - half)))
    return out


def write_out(fb_ref, left_in, column_in, scale_ref, left_ref, right_ref, column_ref, rounded, sem):
    parts = rounded.shape[0]
    copies = [
        pltpu.make_async_copy(left_in, left_ref, sem.at[parts]),
        pltpu.make_async_copy(column_in, column_ref, sem.at[parts + 1]),
    ]
    for copy in copies:
        copy.start()
    n, cz, _ = fb_ref.shape
    rows = n * cz // parts
    for i in range(parts):
        part = fb_ref[pl.ds(i * n // parts, n // parts)].reshape(rows, RANK)
        rounded[i] = (part * scale_ref[...]).astype(jnp.bfloat16)
        copies.append(
            pltpu.make_async_copy(rounded.at[i], right_ref.at[pl.ds(i * rows, rows)], sem.at[i])
        )
        copies[-1].start()
    for copy in copies:
        copy.wait()


def shards(sizes, momentum, previous):
    dn, fn, tn, nr, nc = sizes
    mr, mc = momentum.shape
    wr = mr // dn
    br = wr // tn
    cy = mc // dn
    zn = fn // 2
    cz = cy // zn
    most = pieces_of(cz)[0][0][1]
    width = -(-cy // 128) * 128
    vmem = pltpu.VMEM
    whole = pl.BlockSpec(memory_space=vmem)
    hbm = pl.BlockSpec(memory_space=pl.ANY)
    left, fb, column, scale = pl.pallas_call(
        functools.partial(body, sizes),
        out_shape=(
            jax.ShapeDtypeStruct((mr, RANK), F32),
            jax.ShapeDtypeStruct((dn * zn, cz, RANK), F32),
            jax.ShapeDtypeStruct((1, RANK), F32),
            jax.ShapeDtypeStruct((1, RANK), F32),
        ),
        in_specs=[hbm] * 2,
        out_specs=(whole,) * 4,
        scratch_shapes=[
            vmem((mc, RANK), jnp.bfloat16),
            vmem((wr, mc), F32),
            vmem((mr, width), F32),
            vmem((wr, RANK), F32),
            vmem((tn, br, RANK), F32),
            vmem((mr, RANK), F32),
            vmem((RANK, RANK), F32),
            vmem((fn, RANK // fn, RANK), F32),
            vmem((RANK, RANK), F32),
            vmem((RANK, RANK), F32),
            vmem((RANK, RANK), F32),
            vmem((width, RANK), F32),
            vmem((2, fn, most, RANK), F32),
            vmem((dn * zn, cz, RANK), F32),
            vmem((8, RANK), F32),
            vmem((fn, 8, RANK), F32),
            vmem((8, RANK), F32),
            vmem((tn, 8, RANK), F32),
            pltpu.SemaphoreType.DMA((3,)),
            pltpu.SemaphoreType.DMA((14,)),
            pltpu.SemaphoreType.DMA((14,)),
        ],
        compiler_params=pltpu.CompilerParams(
            collective_id=0, has_side_effects=True, vmem_limit_bytes=LIMIT
        ),
    )(momentum, previous)
    parts = 4 if dn * zn % 4 == 0 and dn * zn * cz // 4 % 16 == 0 else 1
    left, right, column = pl.pallas_call(
        write_out,
        out_shape=(
            jax.ShapeDtypeStruct((mr, RANK), F32),
            jax.ShapeDtypeStruct((mc, RANK), jnp.bfloat16),
            jax.ShapeDtypeStruct((1, RANK), F32),
        ),
        in_specs=[whole] * 4,
        out_specs=(hbm,) * 3,
        scratch_shapes=[
            vmem((parts, mc // parts, RANK), jnp.bfloat16),
            pltpu.SemaphoreType.DMA((parts + 2,)),
        ],
        compiler_params=pltpu.CompilerParams(vmem_limit_bytes=16 * 2**20),
    )(fb, left, column, scale)
    return left, right, column.reshape(RANK)


def solution(mesh):
    dn, fn, tn = (mesh.shape[name] for name in ("dp", "fsdp", "tensor"))

    def run(momentum, previous):
        sizes = (dn, fn, tn, momentum.shape[0], momentum.shape[1])
        return jax.shard_map(
            functools.partial(shards, sizes),
            mesh=mesh,
            in_specs=(P("fsdp", "tensor"), P("tensor", None)),
            out_specs=(P("fsdp", None), P("tensor", None), P()),
            check_vma=False,
        )(momentum, previous)

    return run
```

time: 88.8 us -> 70.3 us (0.79)
  Pallas kernels: 81.5 us -> 68.2 us
  local copies, waits for them, and re-layouts: 6.39 us -> 1.17 us
    pallas_call x1, Pallas kernels: 81.5 us -> 67.2 us  [shards(): pl.pallas_call(functools.partial(body, sizes), out_shape=(jax.ShapeDtypeS...]
    unnamed x7 -> x2, local copies, waits for them, and re-layouts: 6.39 us -> 1.17 us
    pallas_call x0 -> x1, Pallas kernels: none -> 1.06 us  [shards(): pl.pallas_call(write_out, out_shape=(jax.ShapeDtypeStruct((mr, RANK), F32...]
where the time goes in v2:
time: 70.3 us; the launch traced here: 70.1 us
  Pallas kernels  68.2 us (97%)
  local copies, waits for them, and re-layouts  1.17 us (2%)
    pallas_call x1, Pallas kernels, shards(): pl.pallas_call(functools.partial(body, sizes), out_shape=(jax.ShapeDtypeS...  67.2 us

profile of v2, /device:TPU:1, one launch (start us, length us, event | category | flops | bytes accessed | tf_op | source)
XLA Modules:
  0.0 70.1 jit_solution(11710459832896425085)
XLA Ops:
  0.6 0.0 copy-start
  0.6 1.2 %copy-done = bf16[3584,128]{1,0:T(8,128)(2,1)S(1)} copy-done((bf16[3584,128]{1,0:T(8,128)(2,1)S(1)}, bf16[3584,128]{1,0:T(8,128)(2,1)}, u32[]{:S(2)}) %copy-start) | copy-done | bytes 917528
  1.8 67.2 %shard_map.49 = (f32[512,128]{1,0:T(8,128)S(1)}, f32[64,56,128]{2,1,0:T(8,128)S(1)}, f32[1,128]{1,0:T(1,128)S(1)}, f32[1,128]{1,0:T(1,128)S(1)}) custom-call(f32[512,3584]{1,0:T(8,128)} %m_ref.1, bf16[3584,128]{1,0:T(8,128)(2,1)S(1)} %copy-done), custom_call_target="tpu_custom_call" | custom-call | tf_op jit(solution)/shard_map/pallas_call | solution.py:375
  69.0 1.1 %shard_map.50 = (f32[512,128]{1,0:T(8,128)}, bf16[3584,128]{1,0:T(8,128)(2,1)}, f32[1,128]{1,0:T(1,128)}) custom-call(f32[64,56,128]{2,1,0:T(8,128)S(1)} %get-tuple-element.10.fb_ref, f32[512,128]{1,0:T(8,128)S(1)} %get-tuple-element.11.left_in, f32[1,128]{1,0:T(1,128)S(1)} %get-tuple-element.12.column_in, f32[1,128]{1,0:T(1,128)S(1)} %get-tuple-element.13.scale_ref), custom_call_target="tpu_custom_call" | custom-call | tf_op jit(solution)/shard_map/pallas_call | solution.py:413
Async XLA Ops:
  0.6 1.2 %copy-start = (bf16[3584,128]{1,0:T(8,128)(2,1)S(1)}, bf16[3584,128]{1,0:T(8,128)(2,1)}, u32[]{:S(2)}) copy-start(bf16[3584,128]{1,0:T(8,128)(2,1)} %p_ref.1) | copy-start | bytes 2752516

commit v3 on v2

--- a/solution.py
+++ b/solution.py
@@ -80,7 +80,7 @@
 
 def body(
     sizes, m_ref, p_ref, left_ref, fb_ref, column_ref, scale_ref,
-    p_v, mrow, mcol, wpart, rsw, wfull, gpart, rsg, gfull, work, linv, zpart, rsz, zfull, nsend, nrecv, ntotal, nline,
+    p_v, mrow, mcol, turned, wpart, rsw, wfull, gpart, rsg, gfull, work, linv, zpart, rsz, zfull, nsend, nrecv, ntotal, nline,
     load_sem, send_sem, recv_sem,
 ):
     dn, fn, tn, nr, nc = sizes
@@ -112,11 +112,16 @@
         for core in range(2):
             pl.when(c == core)(functools.partial(fun, core, *args))
 
-    lines_x = [at(dx=i) for i in range(1, tn)]
-    lines_y = [at(dy=i) for i in range(1, dn)]
-    lines_f = [at(df=i) for i in range(1, fn)]
-    lines_z = [at(df=2 * i) for i in range(1, zn)]
-    plane = [at(dy=i, dx=j) for i in range(dn) for j in range(tn) if i or j]
+    def far_first(n):
+        return sorted(range(1, n), key=lambda i: -min(i, n - i))
+
+    lines_x = [at(dx=i) for i in far_first(tn)]
+    lines_y = [at(dy=i) for i in far_first(dn)]
+    lines_f = [at(df=i) for i in far_first(fn)]
+    lines_z = [at(df=2 * i) for i in far_first(zn)]
+    plane = [(i, j) for i in range(dn) for j in range(tn) if i or j]
+    plane.sort(key=lambda ij: -(min(ij[0], dn - ij[0]) + min(ij[1], tn - ij[1])))
+    plane = [at(dy=i, dx=j) for i, j in plane]
 
     barrier = pltpu.get_barrier_semaphore()
     for device in lines_x + lines_y + lines_f:
@@ -124,29 +129,36 @@
 
     first_col = (cy * y) // 128 * 128
     skip = aligned(cy * y - first_col)
-    load_p = pltpu.make_async_copy(p_ref, p_v, load_sem.at[0])
-    load_row = pltpu.make_async_copy(m_ref.at[pl.ds(aligned(wr * y), wr)], mrow, load_sem.at[1])
+    step = mc // 7
+    loads = []
+    for i in range(7):
+        part = pl.ds(i * step, step)
+        row = m_ref.at[pl.ds(aligned(wr * y), wr), part]
+        loads.append(
+            (
+                pltpu.make_async_copy(row, mrow.at[:, part], load_sem.at[2 * i]),
+                pltpu.make_async_copy(p_ref.at[part], p_v.at[part], load_sem.at[2 * i + 1]),
+            )
+        )
+        for load in loads[i]:
+            load.start()
     load_col = pltpu.make_async_copy(
-        m_ref.at[:, pl.ds(aligned(first_col, 128), width)], mcol, load_sem.at[2]
+        m_ref.at[:, pl.ds(aligned(first_col, 128), width)], mcol, load_sem.at[14]
     )
-    load_row.start()
-    load_p.start()
     load_col.start()
-    load_row.wait()
-    load_p.wait()
 
     terms = jnp.zeros((3 * wr, RANK), F32)
-    step = 512 if mc % 512 == 0 else 128
-    for i in range(0, mc, step):
-        terms = terms + dot(
-            jnp.concatenate(split(mrow[:, i : i + step]), axis=0), p_v[i : i + step, :], 1, 0
-        )
+    for i in range(7):
+        for load in loads[i]:
+            load.wait()
+        part = slice(i * step, (i + 1) * step)
+        terms = terms + dot(jnp.concatenate(split(mrow[:, part]), axis=0), p_v[part, :], 1, 0)
     wpart[...] = terms[:wr] + (terms[wr : 2 * wr] + terms[2 * wr :])
 
     pl.semaphore_wait(barrier, len(lines_x) + len(lines_y) + len(lines_f))
 
-    for i, device in enumerate(lines_x):
-        to = lax.rem(x + 1 + i, tn)
+    for device in lines_x:
+        to = device[2]
         send(wpart.at[pl.ds(aligned(to * br), br)], rsw.at[x], 0, device)
     rsw[x] = wpart[pl.ds(aligned(x * br), br), :]
     wait(rsw.at[pl.ds(0, tn - 1)], recv_sem.at[0])
@@ -159,23 +171,26 @@
     for device in plane:
         send(wfull.at[pl.ds(mine, br)], wfull.at[pl.ds(mine, br)], 1, device)
     load_col.wait()
+    for i, term in enumerate(split(jnp.transpose(mcol[...]))):
+        turned[i] = term
     wait(wfull.at[pl.ds(0, mr - br)], recv_sem.at[1])
 
     w = wfull[...]
-    gpart[...] = dot(w, w, 0, 0, HIGHEST)
-    for i, device in enumerate(lines_f):
-        to = lax.rem(f + 1 + i, fn)
+    w1, w2, w3 = split(w)
+    t1 = dot(w1, jnp.concatenate([w1, w2, w3, w2], axis=1), 0, 0)
+    t2 = t1[:, RANK : 2 * RANK] + t1[:, 2 * RANK : 3 * RANK]
+    gpart[...] = t1[:, :RANK] + (t2 + jnp.transpose(t2) + dot(w2, w2, 0, 0))
+    for device in lines_f:
+        to = device[1]
         send(gpart.at[pl.ds(aligned(to * gr), gr)], rsg.at[f], 2, device)
     rsg[f] = gpart[pl.ds(aligned(f * gr), gr), :]
 
-    w1, w2, w3 = split(w)
-    m1, m2, m3 = split(mcol[...])
-    t1 = dot(m1, jnp.concatenate([w1, w2, w3, jnp.zeros_like(w1)], axis=1), 0, 0)
-    t2 = dot(m2, jnp.concatenate([w1, w2], axis=1), 0, 0)
-    t3 = t1[:, 2 * RANK : 3 * RANK] + t2[:, RANK:] + dot(m3, w1, 0, 0)
+    t1 = dot(turned[0], jnp.concatenate([w1, w2, w3, jnp.zeros_like(w1)], axis=1), 1, 0)
+    t2 = dot(turned[1], jnp.concatenate([w1, w2], axis=1), 1, 0)
+    t3 = t1[:, 2 * RANK : 3 * RANK] + t2[:, RANK:] + dot(turned[2], w1, 1, 0)
     zpart[...] = t1[:, :RANK] + (t1[:, RANK : 2 * RANK] + t2[:, :RANK] + t3)
     for piece in range(2):
-        for i in range(zn):
+        for i in far_first(zn) + [0]:
             to_z = lax.rem(z + i, zn)
             for core in range(2):
                 start, length = cores[core][piece]
@@ -380,12 +395,13 @@
             jax.ShapeDtypeStruct((1, RANK), F32),
             jax.ShapeDtypeStruct((1, RANK), F32),
         ),
-        in_specs=[hbm] * 2,
+        in_specs=[pl.BlockSpec(memory_space=pltpu.HBM)] * 2,
         out_specs=(whole,) * 4,
         scratch_shapes=[
             vmem((mc, RANK), jnp.bfloat16),
             vmem((wr, mc), F32),
             vmem((mr, width), F32),
+            vmem((3, width, mr), jnp.bfloat16),
             vmem((wr, RANK), F32),
             vmem((tn, br, RANK), F32),
             vmem((mr, RANK), F32),
@@ -401,14 +417,14 @@
             vmem((fn, 8, RANK), F32),
             vmem((8, RANK), F32),
             vmem((tn, 8, RANK), F32),
-            pltpu.SemaphoreType.DMA((3,)),
+            pltpu.SemaphoreType.DMA((15,)),
             pltpu.SemaphoreType.DMA((14,)),
             pltpu.SemaphoreType.DMA((14,)),
         ],
         compiler_params=pltpu.CompilerParams(
             collective_id=0, has_side_effects=True, vmem_limit_bytes=LIMIT
         ),
-    )(momentum, previous)
+    )(pltpu.with_memory_space_constraint(momentum, pltpu.HBM), pltpu.with_memory_space_constraint(previous, pltpu.HBM))
     parts = 4 if dn * zn % 4 == 0 and dn * zn * cz // 4 % 16 == 0 else 1
     left, right, column = pl.pallas_call(
         write_out,

time: 70.3 us -> 67.4 us (0.959)
  Pallas kernels: 68.2 us -> 66.6 us
  local copies, waits for them, and re-layouts: 1.17 us -> 0 us
    pallas_call x1, Pallas kernels: 67.2 us -> 65.5 us  [shards(): pl.pallas_call(functools.partial(body, sizes), out_shape=(jax.ShapeDtypeS...]
    unnamed x2 -> x0, local copies, waits for them, and re-layouts: 1.17 us -> none
where the time goes in v3:
time: 67.4 us; the launch traced here: 67.2 us
  Pallas kernels  66.6 us (99%)
    pallas_call x1, Pallas kernels, shards(): pl.pallas_call(functools.partial(body, sizes), out_shape=(jax.ShapeDtypeS...  65.5 us

profile of v3, /device:TPU:1, one launch (start us, length us, event | category | flops | bytes accessed | tf_op | source)
XLA Modules:
  0.0 67.2 jit_solution(8028991985737677439)
XLA Ops:
  0.6 65.5 %shard_map.49 = (f32[512,128]{1,0:T(8,128)S(1)}, f32[64,56,128]{2,1,0:T(8,128)S(1)}, f32[1,128]{1,0:T(1,128)S(1)}, f32[1,128]{1,0:T(1,128)S(1)}) custom-call(f32[512,3584]{1,0:T(8,128)} %m_ref.1, bf16[3584,128]{1,0:T(8,128)(2,1)} %p_ref.1), custom_call_target="tpu_custom_call" | custom-call | tf_op jit(solution)/shard_map/pallas_call | solution.py:390
  66.2 1.1 %shard_map.50 = (f32[512,128]{1,0:T(8,128)}, bf16[3584,128]{1,0:T(8,128)(2,1)}, f32[1,128]{1,0:T(1,128)}) custom-call(f32[64,56,128]{2,1,0:T(8,128)S(1)} %get-tuple-element.10.fb_ref, f32[512,128]{1,0:T(8,128)S(1)} %get-tuple-element.11.left_in, f32[1,128]{1,0:T(1,128)S(1)} %get-tuple-element.12.column_in, f32[1,128]{1,0:T(1,128)S(1)} %get-tuple-element.13.scale_ref), custom_call_target="tpu_custom_call" | custom-call | tf_op jit(solution)/shard_map/pallas_call | solution.py:429

commit v4 on v3

--- a/solution.py
+++ b/solution.py
@@ -273,23 +273,23 @@
         nsend[...] = jnp.sum((fb * fb).reshape(dn * length // 8, 8, RANK), axis=0)
 
     by_core(squares)
-    for device in lines_f:
-        send(nsend, nrecv.at[f], 10, device)
-    nrecv[f] = nsend[...]
+    for device in lines_x:
+        send(nsend, nline.at[x], 11, device)
+    nline[x] = nsend[...]
     by_core(forward, 1)
 
     left_ref[...] = dot(wfull[...], linv[...] * math.sqrt(nr), 1, 1, HIGHEST)
     l1, l2, l3 = split(jnp.transpose(linv[...]))
     factor = jnp.concatenate([l1, l2, l3, l1, l2, l1], axis=0)
 
-    wait(nrecv.at[pl.ds(0, fn - 1)], recv_sem.at[10])
-    total = nrecv[0]
-    for i in range(1, fn):
-        total = total + nrecv[i]
+    wait(nline.at[pl.ds(0, tn - 1)], recv_sem.at[11])
+    total = nline[0]
+    for i in range(1, tn):
+        total = total + nline[i]
     ntotal[...] = total
-    for device in lines_x:
-        send(ntotal, nline.at[x], 11, device)
-    nline[x] = ntotal[...]
+    for device in lines_f:
+        send(ntotal, nrecv.at[f], 10, device)
+    nrecv[f] = ntotal[...]
 
     other = (y, f + 1 - 2 * c, x)
 
@@ -315,10 +315,10 @@
     by_core(there, 0)
     by_core(here, 1)
 
-    wait(nline.at[pl.ds(0, tn - 1)], recv_sem.at[11])
-    total = nline[0]
-    for i in range(1, tn):
-        total = total + nline[i]
+    wait(nrecv.at[pl.ds(0, fn - 1)], recv_sem.at[10])
+    total = nrecv[0]
+    for i in range(1, fn):
+        total = total + nrecv[i]
     column = jnp.sqrt(jnp.sum(total, axis=0, keepdims=True) + 1e-06)
     column_ref[...] = column / math.sqrt(nc)
     scale_ref[...] = math.sqrt(nc) / column

time: 67.4 us -> 67 us (level)
  no operation moved by 1% of the time
where the time goes in v4:
time: 67 us; the launch traced here: 66.8 us
  Pallas kernels  66.2 us (99%)
    pallas_call x1, Pallas kernels, shards(): pl.pallas_call(functools.partial(body, sizes), out_shape=(jax.ShapeDtypeS...  65.1 us

profile of v4, /device:TPU:1, one launch (start us, length us, event | category | flops | bytes accessed | tf_op | source)
XLA Modules:
  0.0 66.8 jit_solution(2110485724984671570)
XLA Ops:
  0.6 65.1 %shard_map.49 = (f32[512,128]{1,0:T(8,128)S(1)}, f32[64,56,128]{2,1,0:T(8,128)S(1)}, f32[1,128]{1,0:T(1,128)S(1)}, f32[1,128]{1,0:T(1,128)S(1)}) custom-call(f32[512,3584]{1,0:T(8,128)} %m_ref.1, bf16[3584,128]{1,0:T(8,128)(2,1)} %p_ref.1), custom_call_target="tpu_custom_call" | custom-call | tf_op jit(solution)/shard_map/pallas_call | solution.py:390
  65.8 1.1 %shard_map.50 = (f32[512,128]{1,0:T(8,128)}, bf16[3584,128]{1,0:T(8,128)(2,1)}, f32[1,128]{1,0:T(1,128)}) custom-call(f32[64,56,128]{2,1,0:T(8,128)S(1)} %get-tuple-element.10.fb_ref, f32[512,128]{1,0:T(8,128)S(1)} %get-tuple-element.11.left_in, f32[1,128]{1,0:T(1,128)S(1)} %get-tuple-element.12.column_in, f32[1,128]{1,0:T(1,128)S(1)} %get-tuple-element.13.scale_ref), custom_call_target="tpu_custom_call" | custom-call | tf_op jit(solution)/shard_map/pallas_call | solution.py:429
